TPU v7x, 32 devices: a whole 2x2x4 slice. The times are simulated.
32 devices in a mesh: tp: 2 (over x), ep: 16 (over z, y, core).
Axes of the slice: x: 2, y: 2, z: 4, core: 2. Of those that a mesh axis runs over, the one named last changes fastest.
Arguments:
- attn: bfloat16 [8192, 1536], P('ep', 'tp'), may hold values from -6 to 6
- resid: bfloat16 [8192, 1536], P('ep', 'tp'), may hold values from -6 to 6
- w_out: bfloat16 [1536, 1536], P('tp', 'ep'), may hold values from -0.15625 to 0.15625
- gain_mix: float32 [1536], replicated, may hold values from 0.1 to 1.9
- gain_out: float32 [1536], replicated, may hold values from 0.1 to 1.9
- routes: int32 [8192, 8], P('ep'), may hold values from 0 to 39, all different within a row; in each aligned block of 256 rows (0 to 255, 256 to 511, ...) at most 64 rows name the same one
- gates: float32 [8192, 8], P('ep'), may hold values from 0.05 to 1
- w_gate: bfloat16 [48, 1536, 512], P('ep'), as said below
- w_up: bfloat16 [48, 1536, 512], P('ep'), as said below
- w_down: bfloat16 [48, 512, 1536], P('ep'), as said below
Outputs:
- layer_out: bfloat16 [8192, 1536], P('ep', 'tp')
Inputs may be any that keep to these rules, and one draw needn't show every extreme that they name: `routes`: in each aligned block of 256 rows no expert is named more than 64 times; each row names 8 different experts. `w_gate`: copy s holds the weights of expert s % 40. `w_up`: copy s holds the weights of expert s % 40. `w_down`: copy s holds the weights of expert s % 40.
All inputs are finite; a program needn't handle non-finite values.
Results may differ from a plain program's by a relative error of at most 0.0053.
Values may be sent and summed in bfloat16 or wider, within the bound.
A program may use at most 128 MiB of HBM per device.

v0:
```python
import jax
import jax.numpy as jnp
from jax import lax
from jax.sharding import PartitionSpec as P

EXPERTS = 40


epsilon = 1e-05


def rms_scale(values, gain):
    return values * lax.rsqrt(jnp.mean(values * values, axis=1, keepdims=True) + epsilon) * gain


def rank_within(labels, count):
    one_hot = (labels[:, None] == jnp.arange(count, dtype=jnp.int32)[None, :]).astype(jnp.int32)
    before = jnp.cumsum(one_hot, axis=0) - one_hot
    return jnp.sum(before * one_hot, axis=1)


def per_device(attn, resid, w_out, gain_mix, gain_out, routes, gates, w_gate, w_up, w_down):
    tp_count = lax.axis_size("tp")
    tp_rank = lax.axis_index("tp")
    ep_count = lax.axis_size("ep")
    tok_dev = attn.shape[0]
    width_part = attn.shape[1]
    full_width = width_part * tp_count
    rows_here = tok_dev // tp_count
    columns = lax.all_gather(w_out, "ep", axis=1, tiled=True)
    summed = lax.psum_scatter(
        jnp.dot(attn, columns, preferred_element_type=jnp.float32),
        "tp",
        scatter_dimension=1,
        tiled=True,
    )
    hidden = lax.all_to_all(
        resid.astype(jnp.float32) + summed, "tp", split_axis=0, concat_axis=1, tiled=True
    )
    normed = rms_scale(hidden, gain_mix).astype(jnp.bfloat16)
    my_routes = lax.dynamic_slice_in_dim(routes, tp_rank * rows_here, rows_here, 0)
    my_gates = lax.dynamic_slice_in_dim(gates, tp_rank * rows_here, rows_here, 0)
    topk_count = routes.shape[1]
    local_experts = w_gate.shape[0]
    slot_count = local_experts * ep_count
    capacity = rows_here * topk_count // 32
    route_flat = my_routes.reshape(-1)
    rank_e = rank_within(route_flat, EXPERTS)
    target = route_flat * capacity + rank_e
    source_rows = jnp.repeat(normed, topk_count, axis=0)
    send = jnp.zeros((slot_count * capacity, full_width), jnp.bfloat16).at[target].set(source_rows)
    send = send.reshape(ep_count, local_experts, capacity, full_width)
    received = lax.all_to_all(send, "ep", split_axis=0, concat_axis=0, tiled=True)
    gate_pre = jnp.einsum("sfcd,fdh->sfch", received, w_gate, preferred_element_type=jnp.float32)
    up_pre = jnp.einsum("sfcd,fdh->sfch", received, w_up, preferred_element_type=jnp.float32)
    activated = (jax.nn.silu(gate_pre) * up_pre).astype(jnp.bfloat16)
    expert_out = jnp.einsum(
        "sfch,fhd->sfcd", activated, w_down, preferred_element_type=jnp.float32
    ).astype(jnp.bfloat16)
    returned = lax.all_to_all(expert_out, "ep", split_axis=0, concat_axis=0, tiled=True)
    returned = returned.reshape(slot_count * capacity, full_width)
    picked = returned[target].reshape(rows_here, topk_count, full_width)
    combined = hidden + jnp.sum(my_gates[:, :, None] * picked.astype(jnp.float32), axis=1)
    finished = rms_scale(combined, gain_out).astype(jnp.bfloat16)
    return lax.all_to_all(finished, "tp", split_axis=1, concat_axis=0, tiled=True)


def solution(mesh):
    return jax.shard_map(
        per_device,
        mesh=mesh,
        in_specs=(
            P("ep", "tp"),
            P("ep", "tp"),
            P("tp", "ep"),
            P(),
            P(),
            P("ep", None),
            P("ep", None),
            P("ep", None, None),
            P("ep", None, None),
            P("ep", None, None),
        ),
        out_specs=P("ep", "tp"),
        check_vma=False,
    )
```

profile of v0, /device:TPU:12, one launch (start us, length us, event | category | flops | bytes accessed | tf_op | source)
XLA Modules:
  0.0 660.9 jit_solution(4561492879988177996)
XLA Ops:
  6.5 0.0 copy-start
  6.5 0.0 all-gather.2.cloned.1.call-start
  6.5 0.7 all-gather.2.cloned.1.call-update
  7.3 0.0 copy-start.6
  7.3 0.0 reduce-scatter.2.cloned.1.call-start
  7.3 44.2 %all-gather.2.cloned.1.call-done = bf16[768,1536]{0,1:T(8,128)(2,1)} async-done(((bf16[768,96]{0,1:T(8,128)(2,1)}), bf16[768,1536]{0,1:T(8,128)(2,1)}) %all-gather.2.cloned.1.call-update) | async-done | bytes 2359312 | tf_op jit(solution)/shard_map/all_gather | solution.py:30
  51.5 0.0 copy-done
  51.5 4.7 fusion.33
  56.3 0.0 reduce-scatter.2.cloned.1.call-update
  56.3 0.0 copy-done.6
  56.3 0.1 copy.36
  56.5 0.1 eq.29
  56.6 0.1 eq.25
  56.7 11.3 %reduce-window.6 = s32[40,16,128]{2,1,0:T(8,128)S(1)} reduce-window(s32[40,16,128]{2,1,0:T(8,128)S(1)} %fusion.31, s32[]{:T(128)} %constant.9.clone.1), window={size=1x1x128 pad=0_0x0_0x127_0}, to_apply=%region_1.0 | reduce-window | flops 10403840 | bytes 655364 | tf_op jit(solution)/shard_map/reduce-window
  68.1 0.1 slice.10
  68.2 0.3 copy.49
  68.5 0.2 reduce-window.9
  68.7 0.1 copy.35
  68.8 0.1 mul.86
  69.0 31.1 %reduce-scatter.2.cloned.1.call-done = f32[512,768]{1,0:T(8,128)} async-done(((f32[512,1536]{1,0:T(8,128)}), f32[512,768]{1,0:T(8,128)}) %reduce-scatter.2.cloned.1.call-update) | async-done | bytes 1572880 | tf_op jit(solution)/shard_map/reduce_scatter | solution.py:31
  100.1 0.0 copy-done.3
  100.1 1.6 convert_add_fusion
  101.7 0.0 copy-start.4
  101.7 1.6 copy.33
  103.3 3.7 all-to-all-start
  107.0 0.1 broadcast_add_fusion
  107.1 0.1 fusion.30
  107.3 19.1 %all-to-all-done = f32[2,256,768]{1,2,0:T(8,128)S(1)} async-done(((f32[2,256,768]{1,2,0:T(8,128)}), f32[2,256,768]{1,2,0:T(8,128)S(1)}, u32[]{:S(2)}, u32[]{:S(2)}) %all-to-all-start) | async-done | bytes 1572896 | tf_op jit(solution)/shard_map/all_to_all | solution.py:37
  126.5 0.2 fusion.27
  126.7 0.3 fusion.26
  127.0 0.3 copy.40
  127.2 15.5 %scatter_custom_fusion = bf16[3072,1536]{1,0:T(8,128)(2,1)} fusion(s32[2048]{0:T(1024)S(1)} %bitcast.103, bf16[]{:T(256)} %constant.11.clone.1, bf16[256,1536]{1,0:T(8,128)(2,1)S(1)} %copy.40), kind=kCustom, calls=%fused_computation.16 | custom fusion | bytes 10223618 | tf_op jit(solution)/shard_map/scatter | solution.py:51
  142.7 210.5 %all_to_all.45 = bf16[16,3,64,1536]{3,2,1,0:T(8,128)(2,1)S(1)} all-to-all(bf16[16,3,64,1536]{3,2,1,0:T(8,128)(2,1)} %bitcast.94), channel_id=1, replica_groups=mesh['tp'=2,'ep'=16] {'ep'}, dimensions={0} | all-to-all | bytes 18874368 | tf_op jit(solution)/shard_map/all_to_all | solution.py:53
  353.3 3.7 copy-done.2
  356.9 9.3 %fusion.1 = f32[3,16,64,512]{3,2,1,0:T(8,128)} fusion(bf16[16,3,64,1536]{3,2,1,0:T(8,128)(2,1)S(1)} %all_to_all.45, bf16[3,1536,512]{2,1,0:T(8,128)(2,1)} %param.18), kind=kOutput, calls=%fused_computation.5 | convolution fusion | flops 4831838208 | bytes 20447232 | tf_op jit(solution)/shard_map/sfcd,fdh->sfch/dot_general | solution.py:55
  366.2 18.9 %convert_bitcast_fusion = bf16[16,3,64,1536]{3,2,0,1:T(8,128)(2,1)} fusion(bf16[3,512,1536]{2,1,0:T(8,128)(2,1)} %param.19, f32[3,16,64,512]{3,2,1,0:T(8,128)} %fusion.1, bf16[3,1536,512]{2,1,0:T(8,128)(2,1)} %param.17, bf16[16,3,64,1536]{3,2,1,0:T(8,128)(2,1)} %copy-done.2), kind=kOutput, calls=%fused_computation.4 | convolution fusion | flops 9677832192 | bytes 34603008 | tf_op jit(solution)/shard_map/sfch,fhd->sfcd/dot_general | solution.py:57
  385.2 8.4 %copy.43 = bf16[16,3,64,1536]{3,2,1,0:T(8,128)(2,1)} copy(bf16[16,3,64,1536]{3,2,0,1:T(8,128)(2,1)} %convert_bitcast_fusion) | data formatting | bytes 18874368 | tf_op jit(solution)/shard_map/convert_element_type | solution.py:59
  393.6 6.1 all-to-all-start.2
  399.7 0.1 copy.34
  399.9 204.5 %all-to-all-done.2 = bf16[16,3,64,1536]{3,2,1,0:T(8,128)(2,1)} async-done(((bf16[16,3,64,1536]{3,2,1,0:T(8,128)(2,1)}), bf16[16,3,64,1536]{3,2,1,0:T(8,128)(2,1)}, u32[]{:S(2)}, u32[]{:S(2)}) %all-to-all-start.2) | async-done | bytes 9437216 | tf_op jit(solution)/shard_map/all_to_all | solution.py:60
  604.4 18.2 %gather_fusion = bf16[2048,1536]{1,0:T(8,128)(2,1)} fusion(bf16[3072,1536]{1,0:T(8,128)(2,1)} %bitcast.19, s32[2048]{0:T(1024)S(1)} %broadcast_clamp_fusion), kind=kCustom, calls=%fused_computation | custom fusion | bytes 12591104 | tf_op jit(solution)/shard_map/gather | solution.py:62
  622.5 10.0 %fusion = f32[256,1536]{1,0:T(8,128)} fusion(bf16[2048,1536]{1,0:T(8,128)(2,1)} %gather_fusion, f32[256,8]{1,0:T(8,128)S(1)} %copy.34), kind=kLoop, calls=%fused_computation.3 | loop fusion | flops 9043968 | bytes 7872512 | tf_op jit(solution)/shard_map/reduce_sum | solution.py:63
  632.5 3.0 copy.44
  635.6 1.7 multiply_reduce_fusion
  637.3 1.7 multiply_convert_fusion
  639.0 14.0 %all_to_all.46 = bf16[256,2,768]{0,2,1:T(8,128)(2,1)S(1)} all-to-all(bf16[256,2,768]{0,2,1:T(8,128)(2,1)S(1)} %multiply_convert_fusion), channel_id=1, replica_groups=mesh['tp'=2,'ep'=16] {'tp'}, dimensions={1} | all-to-all | bytes 1572864 | tf_op jit(solution)/shard_map/all_to_all | solution.py:65
  652.9 1.2 copy.45
  654.1 0.0 copy-done.1
  (16 shorter events, 0.1 us)
Async XLA Ops:
  6.5 45.0 %copy-start = (bf16[512,768]{1,0:T(8,128)(2,1)S(1)}, bf16[512,768]{1,0:T(8,128)(2,1)}, u32[]{:S(2)}) copy-start(bf16[512,768]{1,0:T(8,128)(2,1)} %param.10) | copy-start | bytes 2359300
  6.5 45.0 %all-gather.2.cloned.1.call-start = ((), (), s32[]{:S(2)}) async-start(), calls=%async_computation.5 | async-start | bytes 2506752 | tf_op jit(solution)/shard_map/all_gather | solution.py:30
  7.3 49.1 %copy-start.6 = (s32[512,8]{0,1:T(8,128)S(1)}, s32[512,8]{0,1:T(8,128)}, u32[]{:S(2)}) copy-start(s32[512,8]{0,1:T(8,128)} %param.15) | copy-start | bytes 49156
  7.3 92.8 %reduce-scatter.2.cloned.1.call-start = ((), (), s32[]{:S(2)}) async-start(), calls=%async_computation.6 | async-start | bytes 4718592 | tf_op jit(solution)/shard_map/reduce_scatter | solution.py:31
  56.3 43.8 %copy-start.3 = (bf16[512,768]{1,0:T(8,128)(2,1)S(1)}, bf16[512,768]{1,0:T(8,128)(2,1)}, u32[]{:S(2)}) copy-start(bf16[512,768]{1,0:T(8,128)(2,1)} %param.11) | copy-start | bytes 2359300
  101.7 25.0 %copy-start.4 = (f32[1536]{0:T(1024)S(1)}, f32[1536]{0:T(1024)}, u32[]{:S(2)}) copy-start(f32[1536]{0:T(1024)} %param.13) | copy-start | bytes 18436
  103.3 23.2 %all-to-all-start = ((f32[2,256,768]{1,2,0:T(8,128)}), f32[2,256,768]{1,2,0:T(8,128)S(1)}, u32[]{:S(2)}, u32[]{:S(2)}) async-start(f32[2,256,768]{1,2,0:T(8,128)} %copy.33), calls=%async_computation.1 | async-start | bytes 3145728 | tf_op jit(solution)/shard_map/all_to_all | solution.py:37
  353.3 3.7 copy-start.2
  393.6 6.1 copy-start.7
  393.6 6.3 copy-start.5
  393.6 210.8 %all-to-all-start.2 = ((bf16[16,3,64,1536]{3,2,1,0:T(8,128)(2,1)}), bf16[16,3,64,1536]{3,2,1,0:T(8,128)(2,1)}, u32[]{:S(2)}, u32[]{:S(2)}) async-start(bf16[16,3,64,1536]{3,2,1,0:T(8,128)(2,1)} %copy.43), calls=%async_computation.3 | async-start | bytes 18874368 | tf_op jit(solution)/shard_map/all_to_all | solution.py:60
  635.6 18.5 %copy-start.1 = (bf16[512,768]{1,0:T(8,128)(2,1)S(1)}, bf16[512,768]{1,0:T(8,128)(2,1)}, u32[]{:S(2)}) copy-start(bf16[512,768]{1,0:T(8,128)(2,1)} %param.10) | copy-start | bytes 2359300
Sparse Core Ops, SparseCore 0:
  9.6 41.8 all-gather.1
  56.4 43.6 reduce-scatter.1
where the time goes:
time: 662 us; the launch traced here: 661 us
  waiting for transfers between devices  300 us (45%)
  blocking collectives  224 us (34%)
  local copies, waits for them, and re-layouts  53 us (8%)
  matrix products  33 us (5%)
  other arithmetic  27.4 us (4%)
  between operations  13.6 us (2%)
  starting transfers between devices  9.83 us (1%)
    all_to_all x1, blocking collectives, per_device(): lax.all_to_all(send, 'ep', split_axis=0, concat_axis=0, tiled=True)  211 us
    all_to_all x1, waiting for transfers between devices, per_device(): lax.all_to_all(expert_out, 'ep', split_axis=0, concat_axis=0, tiled=True)  204 us
    all_gather x1, waiting for transfers between devices, per_device(): columns = lax.all_gather(w_out, 'ep', axis=1, tiled=True)  44.2 us
    reduce_scatter x1, waiting for transfers between devices, per_device(): lax.psum_scatter(jnp.dot(attn, columns, preferred_element_type=jnp.float3...  31.1 us
    all_to_all x1, waiting for transfers between devices, per_device(): lax.all_to_all(resid.astype(jnp.float32) + summed, 'tp', split_axis=0, co...  19.1 us
    dot_general x1, matrix products, per_device(): jnp.einsum('sfch,fhd->sfcd', activated, w_down, preferred_element_type=jn...  18.9 us
    gather x1, local copies, waits for them, and re-layouts, per_device(): picked = returned[target].reshape(rows_here, topk_count, full_width)  18.2 us
    scatter x1, local copies, waits for them, and re-layouts, per_device(): jnp.zeros((slot_count * capacity, full_width), jnp.bfloat16).at[target]  15.5 us
  transfers between devices with their start and end apart: 4, of which 4 were waited for; matrix products, arithmetic and copies ran while one was open for 2% of the time, Pallas kernels for 0%

commit v1 on v0

v1 whole, which is shorter than its diff:
```python
import functools

import jax
import jax.numpy as jnp
from jax import lax
from jax.experimental import pallas as pl
from jax.experimental.pallas import tpu as pltpu
from jax.sharding import PartitionSpec as P

EXPERTS = 40
EPSILON = 1e-05
CHUNKS = 2
MESH = pl.DeviceIdType.MESH


def chip_at(place, chips):
    far = place // (chips // 2)
    return (1 - far) * (2 * place) + far * (2 * (chips - 1 - place) + 1)


def place_of(chip, chips):
    odd = chip % 2
    return (1 - odd) * (chip // 2) + odd * (chips - 1 - chip // 2)


def layer_kernel(
    tp_count, chips, rows, width, local, cap, split_out,
    parts_ref, own_ref, table_ref, gain_mix_ref, gain_out_ref, gate_hbm, up_hbm, down_hbm,
    out_ref,
    tokens, sums, away, from_pair, from_prev, from_next, hidden, part_in, w_gate, w_up, w_down,
    picked, pick_mats, scaled, finished,
    weight_sem, part_send, part_recv, right_send, right_recv, left_send, left_recv,
    pair_send, pair_recv, down_send, down_recv, back_send, back_recv, cross_send, cross_recv,
    out_send, out_recv,
):
    half = chips // 2
    step_rows = rows // CHUNKS
    mid = width // 2
    ep = lax.axis_index("ep")
    tp = lax.axis_index("tp")
    core = ep % 2
    place = place_of(ep // 2, chips)
    after = chip_at((place + 1) % chips, chips) * 2 + core
    before = chip_at((place + chips - 1) % chips, chips) * 2 + core
    pair = ep + 1 - 2 * core

    barrier = pltpu.get_barrier_semaphore()
    for other in (after, before, pair):
        pl.semaphore_signal(barrier, inc=1, device_id={"ep": other}, device_id_type=MESH)
    for k in range(1, tp_count):
        pl.semaphore_signal(barrier, inc=1, device_id={"tp": (tp + k) % tp_count}, device_id_type=MESH)
    pl.semaphore_wait(barrier, 3 + tp_count - 1)

    loads = [
        pltpu.make_async_copy(src, dst, weight_sem.at[i])
        for i, (src, dst) in enumerate(((gate_hbm, w_gate), (up_hbm, w_up), (down_hbm, w_down)))
    ]

    def to_ep(src, dst, send, recv, other):
        return pltpu.make_async_remote_copy(
            src_ref=src, dst_ref=dst, send_sem=send, recv_sem=recv,
            device_id={"ep": other}, device_id_type=MESH)

    def to_tp(src, dst, send, recv, k):
        return pltpu.make_async_remote_copy(
            src_ref=src, dst_ref=dst, send_sem=send, recv_sem=recv,
            device_id={"tp": (tp + k) % tp_count}, device_id_type=MESH)

    def band(c):
        return pl.ds(c * step_rows, step_rows)

    def part_copy(k, c):
        return to_tp(parts_ref.at[(tp + k) % tp_count, band(c)], part_in.at[k - 1, band(c)],
                     part_send.at[k - 1, c], part_recv.at[k - 1, c], k)

    for c in range(CHUNKS):
        for k in range(1, tp_count):
            part_copy(k, c).start()
    for load in loads:
        load.start()

    def right_copy(t, c):
        return to_ep(tokens.at[t - 1, 0, band(c)], tokens.at[t, 0, band(c)],
                     right_send.at[t - 1, c], right_recv.at[t - 1, c], after)

    def left_copy(t, c):
        return to_ep(tokens.at[(chips - t + 1) % chips, 0, band(c)], tokens.at[chips - t, 0, band(c)],
                     left_send.at[t - 1, c], left_recv.at[t - 1, c], before)

    def right_last(c):
        return to_ep(tokens.at[half - 1, 0, band(c), pl.ds(0, mid)], tokens.at[half, 0, band(c), pl.ds(0, mid)],
                     right_send.at[half - 1, c], right_recv.at[half - 1, c], after)

    def left_last(c):
        return to_ep(tokens.at[half + 1, 0, band(c), pl.ds(mid, mid)], tokens.at[half, 0, band(c), pl.ds(mid, mid)],
                     left_send.at[half - 1, c], left_recv.at[half - 1, c], before)

    def pair_copy(s, c):
        return to_ep(tokens.at[s, 0, band(c)], tokens.at[s, 1, band(c)],
                     pair_send.at[s, c], pair_recv.at[s, c], pair)

    small = min(32, step_rows)

    def norm_rows(at, gain_ref, add):
        value = add(at)
        scale = lax.rsqrt(jnp.mean(value * value, axis=1, keepdims=True) + EPSILON)
        return value, (value * scale * gain_ref[...]).astype(jnp.bfloat16)

    for c in range(CHUNKS):
        for k in range(1, tp_count):
            part_copy(k, c).wait_recv()

        def mix(i, carry):
            at = pl.ds(pl.multiple_of(c * step_rows + i * small, small), small)

            def add(at):
                value = own_ref[at, :]
                for k in range(1, tp_count):
                    value = value + part_in[k - 1, at, :].astype(jnp.float32)
                return value

            value, normed = norm_rows(at, gain_mix_ref, add)
            hidden[at, :] = value
            tokens[0, 0, at, :] = normed
            return carry

        lax.fori_loop(0, step_rows // small, mix, 0)
        right_copy(1, c).start()
        left_copy(1, c).start()
        pair_copy(0, c).start()
    for load in loads:
        load.wait()

    def experts(blocks):
        where = []
        for slot, which, _ in blocks:
            chip = chip_at((place + chips - slot) % chips, chips)
            where.append(chip * 2 + (core + which - 2 * core * which))
        count = len(blocks)

        def one(f, carry):
            at = pl.ds(pl.multiple_of(f * cap, cap), cap)
            columns = []
            for b, (slot, which, _) in enumerate(blocks):
                place_row = table_ref[where[b], pl.ds(f, 1), :]
                gate_row = table_ref[where[b], pl.ds(local + f, 1), :]
                index = lax.broadcasted_iota(jnp.int32, (cap, rows), 0).astype(jnp.float32)
                hit = index == place_row
                columns.append(jnp.sum(jnp.where(hit, gate_row, 0.0), axis=1, keepdims=True))
                choose = jnp.where(hit, 1.0, 0.0).astype(jnp.bfloat16)
                pick_mats[b, at, :] = choose
                picked[pl.ds(b * cap, cap), :] = jnp.dot(
                    choose, tokens[slot, which], preferred_element_type=jnp.float32).astype(jnp.bfloat16)
            rows_in = picked[pl.ds(0, count * cap), :]
            gate = jnp.dot(rows_in, w_gate[f], preferred_element_type=jnp.float32)
            up = jnp.dot(rows_in, w_up[f], preferred_element_type=jnp.float32)
            act = (gate / (1.0 + jnp.exp(-gate)) * up).astype(jnp.bfloat16)
            result = jnp.dot(act, w_down[f], preferred_element_type=jnp.float32)
            for b in range(count):
                scaled[b, at, :] = (result[b * cap:(b + 1) * cap, :] * columns[b]).astype(jnp.bfloat16)
            return carry

        lax.fori_loop(0, local, one, 0)
        for b, (_, _, target) in enumerate(blocks):
            target[...] = lax.dot_general(
                pick_mats[b], scaled[b], (((0,), (0,)), ((), ())),
                preferred_element_type=jnp.float32).astype(jnp.bfloat16)

    def cross_copy(s, buffer):
        return to_ep(away.at[buffer], from_pair.at[s], cross_send.at[s], cross_recv.at[s], pair)

    def step(t, carry):
        for c in range(CHUNKS):
            right_copy(t, c).wait_recv()

            @pl.when(t < half - 1)
            def _():
                right_copy(t + 1, c).start()

            @pl.when(t == half - 1)
            def _():
                right_last(c).start()

            pair_copy(t, c).start()
            left_copy(t, c).wait_recv()

            @pl.when(t < half - 1)
            def _():
                left_copy(t + 1, c).start()

            @pl.when(t == half - 1)
            def _():
                left_last(c).start()

            pair_copy(chips - t, c).start()
        for c in range(CHUNKS):
            pair_copy(t, c).wait_recv()
            pair_copy(chips - t, c).wait_recv()
        turn = t % 2

        @pl.when(t > 2)
        def _():
            cross_copy(t - 2, 2 * turn).wait_send()
            cross_copy(chips - t + 2, 2 * turn + 1).wait_send()

        experts([
            (t, 0, sums.at[t]), (t, 1, away.at[2 * turn]),
            (chips - t, 0, sums.at[chips - t]), (chips - t, 1, away.at[2 * turn + 1]),
        ])
        cross_copy(t, 2 * turn).start()
        cross_copy(chips - t, 2 * turn + 1).start()
        return carry

    lax.fori_loop(1, half, step, 0)

    for c in range(CHUNKS):
        right_last(c).wait_recv()
        left_last(c).wait_recv()
        pair_copy(half, c).start()
    for c in range(CHUNKS):
        pair_copy(half, c).wait_recv()
    turn_a, turn_b = half % 2, (half - 1) % 2
    if half > 2:
        cross_copy(half - 2, 2 * turn_a).wait_send()
        cross_copy(chips - half + 2, 2 * turn_a + 1).wait_send()
    experts([(half, 0, sums.at[half]), (half, 1, away.at[2 * turn_a])])
    cross_copy(half, 2 * turn_a).start()

    def add_rows(s, at, extra, columns=slice(None)):
        def body(i, carry):
            here = pl.ds(pl.multiple_of(at + i * small, small), small)
            value = sums[s, here, columns].astype(jnp.float32) + from_pair[s, here, columns].astype(jnp.float32)
            if extra is not None:
                value = value + extra[here, columns].astype(jnp.float32)
            sums[s, here, columns] = value.astype(jnp.bfloat16)
            return carry

        lax.fori_loop(0, step_rows // small, body, 0)

    def down_first(c):
        return to_ep(sums.at[half, band(c), pl.ds(0, mid)], from_prev.at[half - 1, band(c), pl.ds(0, mid)],
                     down_send.at[half - 1, c], down_recv.at[half - 1, c], after)

    def back_first(c):
        return to_ep(sums.at[half, band(c), pl.ds(mid, mid)], from_next.at[half - 1, band(c), pl.ds(mid, mid)],
                     back_send.at[half - 1, c], back_recv.at[half - 1, c], before)

    def down_copy(t, c):
        return to_ep(sums.at[chips - t, band(c)], from_prev.at[t - 1, band(c)],
                     down_send.at[t - 1, c], down_recv.at[t - 1, c], after)

    def back_copy(t, c):
        return to_ep(sums.at[t, band(c)], from_next.at[t - 1, band(c)],
                     back_send.at[t - 1, c], back_recv.at[t - 1, c], before)

    cross_copy(half, 2 * turn_a).wait_recv()
    for c in range(CHUNKS):
        add_rows(half, c * step_rows, None)
        down_first(c).start()
        back_first(c).start()

    for c in range(CHUNKS):
        pair_copy(0, c).wait_recv()
    cross_copy(half - 1, 2 * turn_b).wait_send()
    cross_copy(chips - half + 1, 2 * turn_b + 1).wait_send()
    experts([(0, 0, sums.at[0]), (0, 1, away.at[2 * turn_b])])
    cross_copy(0, 2 * turn_b).start()

    last = half - 1
    cross_copy(last, 0).wait_recv()
    cross_copy(chips - last, 0).wait_recv()
    for c in range(CHUNKS):
        down_first(c).wait_recv()
        add_rows(chips - last, c * step_rows, from_prev.at[last], pl.ds(0, mid))
        add_rows(chips - last, c * step_rows, None, pl.ds(mid, mid))
        down_copy(last, c).start()
        back_first(c).wait_recv()
        add_rows(last, c * step_rows, None, pl.ds(0, mid))
        add_rows(last, c * step_rows, from_next.at[last], pl.ds(mid, mid))
        back_copy(last, c).start()

    def sum_step(i, carry):
        t = half - 2 - i
        cross_copy(t, 0).wait_recv()
        cross_copy(chips - t, 0).wait_recv()
        for c in range(CHUNKS):
            down_copy(t + 1, c).wait_recv()
            add_rows(chips - t, c * step_rows, from_prev.at[t])
            down_copy(t, c).start()
            back_copy(t + 1, c).wait_recv()
            add_rows(t, c * step_rows, from_next.at[t])
            back_copy(t, c).start()
        return carry

    lax.fori_loop(0, half - 2, sum_step, 0)
    cross_copy(0, 0).wait_recv()

    part_width = width // tp_count

    def out_copy(k, c):
        at = pl.ds(tp * rows + c * step_rows, step_rows)
        return to_tp(finished.at[(tp + k) % tp_count, band(c)], out_ref.at[at],
                     out_send.at[k - 1, c], out_recv.at[k - 1, c], k)

    for c in range(CHUNKS):
        down_copy(1, c).wait_recv()
        back_copy(1, c).wait_recv()

        def close(i, carry):
            at = pl.ds(pl.multiple_of(c * step_rows + i * small, small), small)

            def add(at):
                value = hidden[at, :]
                for part in (sums.at[0], from_pair.at[0], from_prev.at[0], from_next.at[0]):
                    value = value + part[at, :].astype(jnp.float32)
                return value

            _, done = norm_rows(at, gain_out_ref, add)
            if split_out:
                for r in range(tp_count):
                    finished[r, at, :] = done[:, r * part_width:(r + 1) * part_width]
            else:
                out_ref[at, :] = done
            return carry

        lax.fori_loop(0, step_rows // small, close, 0)
        if split_out:
            for k in range(1, tp_count):
                out_copy(k, c).start()

            def keep(i, carry):
                at = pl.multiple_of(c * step_rows + i * small, small)
                out_ref[pl.ds(tp * rows + at, small), :] = finished[tp, pl.ds(at, small), :]
                return carry

            lax.fori_loop(0, step_rows // small, keep, 0)

    for c in range(CHUNKS):
        for k in range(1, tp_count):
            part_copy(k, c).wait_send()
            if split_out:
                out_copy(k, c).wait_send()
                out_copy(k, c).wait_recv()
        right_last(c).wait_send()
        left_last(c).wait_send()
        down_first(c).wait_send()
        back_first(c).wait_send()

    def drain(i, carry):
        t = i + 1
        for c in range(CHUNKS):
            right_copy(t, c).wait_send()
            left_copy(t, c).wait_send()
            down_copy(t, c).wait_send()
            back_copy(t, c).wait_send()
        return carry

    lax.fori_loop(0, half - 1, drain, 0)

    def drain_pair(s, carry):
        for c in range(CHUNKS):
            pair_copy(s, c).wait_send()
        return carry

    lax.fori_loop(0, chips, drain_pair, 0)
    cross_copy(half, 2 * turn_a).wait_send()
    cross_copy(0, 2 * turn_b).wait_send()


def per_device(attn, resid, w_out, gain_mix, gain_out, routes, gates, w_gate, w_up, w_down):
    tp_count = lax.axis_size("tp")
    tp_rank = lax.axis_index("tp")
    ep_count = lax.axis_size("ep")
    ep_rank = lax.axis_index("ep")
    tok_dev, width_part = attn.shape
    width = width_part * tp_count
    rows = tok_dev // tp_count
    topk = routes.shape[1]
    local, _, hidden_units = w_gate.shape
    cap = rows * topk // 32
    chips = ep_count // 2
    half = chips // 2
    split_out = width_part % 128 == 0

    my_routes = lax.dynamic_slice_in_dim(routes, tp_rank * rows, rows, 0)
    my_gates = lax.dynamic_slice_in_dim(gates, tp_rank * rows, rows, 0)
    both = jnp.concatenate([my_routes.T.astype(jnp.float32), my_gates.T], axis=0)
    both = lax.all_gather(both, "ep", axis=0)
    slot = ep_rank * local + jnp.arange(local, dtype=jnp.int32)
    expert = jnp.where(slot < EXPERTS, slot, -1).astype(jnp.float32)
    named = both[:, None, :topk, :] == expert[None, :, None, None]
    hit = jnp.any(named, axis=2)
    weight = jnp.sum(jnp.where(named, both[:, None, topk:, :], 0.0), axis=2)
    earlier = jnp.triu(jnp.ones((rows, rows), jnp.bfloat16), 1)
    rank = jnp.einsum("bfi,ij->bfj", hit.astype(jnp.bfloat16), earlier, preferred_element_type=jnp.float32)
    table = jnp.concatenate([jnp.where(hit, rank, -1.0), weight], axis=1)
    table = jnp.pad(table, ((0, 0), (0, -(2 * local) % 8), (0, 0)))

    columns = lax.all_gather(w_out, "ep", axis=1, tiled=True)
    part = jnp.dot(attn, columns, preferred_element_type=jnp.float32)
    spread = lax.dynamic_update_slice(jnp.zeros((tok_dev, width), resid.dtype), resid, (0, tp_rank * width_part))
    part = part + spread.astype(jnp.float32)
    own = lax.dynamic_slice_in_dim(part, tp_rank * rows, rows, 0)
    parts = part.astype(jnp.bfloat16).reshape(tp_count, rows, width)

    bf16, f32 = jnp.bfloat16, jnp.float32
    vmem = pl.BlockSpec(memory_space=pltpu.VMEM)
    anywhere = pl.BlockSpec(memory_space=pl.ANY)
    dma = pltpu.SemaphoreType.DMA
    others = tp_count - 1
    out_shape = (tok_dev, width_part) if split_out else (rows, width)
    result = pl.pallas_call(
        functools.partial(layer_kernel, tp_count, chips, rows, width, local, cap, split_out),
        out_shape=jax.ShapeDtypeStruct(out_shape, bf16),
        in_specs=[vmem] * 5 + [anywhere] * 3,
        out_specs=vmem,
        scratch_shapes=[
            pltpu.VMEM((chips, 2, rows, width), bf16),
            pltpu.VMEM((chips, rows, width), bf16),
            pltpu.VMEM((4, rows, width), bf16),
            pltpu.VMEM((chips, rows, width), bf16),
            pltpu.VMEM((half, rows, width), bf16),
            pltpu.VMEM((half, rows, width), bf16),
            pltpu.VMEM((rows, width), f32),
            pltpu.VMEM((others, rows, width), bf16),
            pltpu.VMEM(w_gate.shape, bf16),
            pltpu.VMEM(w_up.shape, bf16),
            pltpu.VMEM(w_down.shape, bf16),
            pltpu.VMEM((4 * cap, width), bf16),
            pltpu.VMEM((4, local * cap, rows), bf16),
            pltpu.VMEM((4, local * cap, width), bf16),
            pltpu.VMEM((tp_count, rows, width_part), bf16),
            dma((3,)),
            dma((others, CHUNKS)), dma((others, CHUNKS)),
            dma((half, CHUNKS)), dma((half, CHUNKS)),
            dma((half, CHUNKS)), dma((half, CHUNKS)),
            dma((chips, CHUNKS)), dma((chips, CHUNKS)),
            dma((half, CHUNKS)), dma((half, CHUNKS)),
            dma((half, CHUNKS)), dma((half, CHUNKS)),
            dma((chips,)), dma((chips,)),
            dma((others, CHUNKS)), dma((others, CHUNKS)),
        ],
        compiler_params=pltpu.CompilerParams(
            collective_id=0, has_side_effects=True, vmem_limit_bytes=63 * 1024 * 1024),
    )(parts, own, table, gain_mix.reshape(1, width), gain_out.reshape(1, width), w_gate, w_up, w_down)
    if split_out:
        return result
    return lax.all_to_all(result, "tp", split_axis=1, concat_axis=0, tiled=True)


def solution(mesh):
    return jax.shard_map(
        per_device,
        mesh=mesh,
        in_specs=(
            P("ep", "tp"),
            P("ep", "tp"),
            P("tp", "ep"),
            P(),
            P(),
            P("ep", None),
            P("ep", None),
            P("ep", None, None),
            P("ep", None, None),
            P("ep", None, None),
        ),
        out_specs=P("ep", "tp"),
        check_vma=False,
    )
```

time: 662 us -> 224 us (0.34)
  waiting for transfers between devices: 300 us -> 23.9 us
  blocking collectives: 224 us -> 15.8 us
  Pallas kernels: 0 us -> 155 us
  local copies, waits for them, and re-layouts: 53 us -> 6.81 us
  matrix products: 33 us -> 4.38 us
  other arithmetic: 27.4 us -> 1.87 us
  starting transfers between devices: 9.83 us -> 0.01 us
    all_to_all x2 -> x0, blocking collectives: 224 us -> none  [the longest x1 211 us: per_device(): lax.all_to_all(send, 'ep', split_axis=0, concat_axis=0, tiled=True)]
    all_to_all x2 -> x0, waiting for transfers between devices: 224 us -> none  [the longest x1 204 us: per_device(): lax.all_to_all(expert_out, 'ep', split_axis=0, concat_axis=0, tiled=True)]
    pallas_call x0 -> x1, Pallas kernels: none -> 155 us  [per_device(): pl.pallas_call(functools.partial(layer_kernel, tp_count, chips, rows, wid...]
    reduce_scatter x1 -> x0, waiting for transfers between devices: 31.1 us -> none  [per_device(): lax.psum_scatter(jnp.dot(attn, columns, preferred_element_type=jnp.float3...]
    dot_general x3 -> x2, matrix products: 33 us -> 4.38 us  [the longest x1 4.24 us: per_device(): part = jnp.dot(attn, columns, preferred_element_type=jnp.float32)]
    all_gather x1, waiting for transfers between devices: 44.2 us -> 23.2 us  [per_device(): columns = lax.all_gather(w_out, 'ep', axis=1, tiled=True)]
    gather x1 -> x0, local copies, waits for them, and re-layouts: 18.2 us -> none  [per_device(): picked = returned[target].reshape(rows_here, topk_count, full_width)]
    all_gather x0 -> x1, blocking collectives: none -> 15.8 us  [per_device(): both = lax.all_gather(both, 'ep', axis=0)]
  transfers between devices with their start and end apart: 4 -> 1, of which waited for: 4 -> 1; matrix products, arithmetic and copies ran while one was open for 2% -> 2% of each run, Pallas kernels for 0% -> 0%
where the time goes in v1:
time: 224 us; the launch traced here: 221 us
  Pallas kernels  155 us (69%)
  waiting for transfers between devices  23.9 us (11%)
  blocking collectives  15.8 us (7%)
  between operations  13.4 us (6%)
  local copies, waits for them, and re-layouts  6.81 us (3%)
  matrix products  4.38 us (2%)
    pallas_call x1, Pallas kernels, per_device(): pl.pallas_call(functools.partial(layer_kernel, tp_count, chips, rows, wid...  155 us
    all_gather x1, waiting for transfers between devices, per_device(): columns = lax.all_gather(w_out, 'ep', axis=1, tiled=True)  23.2 us
    all_gather x1, blocking collectives, per_device(): both = lax.all_gather(both, 'ep', axis=0)  15.8 us
  transfers between devices with their start and end apart: 1, of which 1 were waited for; matrix products, arithmetic and copies ran while one was open for 2% of the time, Pallas kernels for 0%

profile of v1, /device:TPU:12, one launch (start us, length us, event | category | flops | bytes accessed | tf_op | source)
XLA Modules:
  0.0 221.5 jit_solution(13525381985246306435)
XLA Ops:
  6.5 0.0 copy-start
  6.5 0.0 copy-start.1
  6.5 0.0 all-gather.3.cloned.1.call-start
  6.5 0.7 all-gather.3.cloned.1.call-update
  7.3 1.3 reshape.19.gain_mix_ref
  8.6 1.3 reshape.20.gain_out_ref
  9.9 0.7 dynamic-slice_bitcast_fusion
  10.6 0.7 convert_bitcast_fusion
  11.3 15.8 %all-gather = f32[256,256]{1,0:T(8,128)S(1)} all-gather(f32[16,256]{1,0:T(8,128)S(1)} %pad_maximum_fusion), channel_id=2, replica_groups=mesh['tp'=2,'ep'=16] {'ep'}, dimensions={0}, use_global_device_ids=true | all-gather | bytes 278528 | tf_op jit(solution)/shard_map/all_gather | solution.py:388
  27.1 0.2 compare_reduce_fusion
  27.3 0.2 fusion
  27.5 0.1 fusion.3
  27.7 0.1 copy_select_fusion
  27.8 0.7 select_maximum_fusion.table_ref
  28.5 0.1 broadcast_in_dim.33
  28.6 0.0 copy-done.1
  28.6 0.1 constant_dynamic-update-slice_fusion
  28.6 23.2 %all-gather.3.cloned.1.call-done = bf16[768,1536]{0,1:T(8,128)(2,1)} async-done(((bf16[768,96]{0,1:T(8,128)(2,1)}), bf16[768,1536]{0,1:T(8,128)(2,1)}) %all-gather.3.cloned.1.call-update) | async-done | bytes 2359312 | tf_op jit(solution)/shard_map/all_gather | solution.py:399
  51.8 0.0 copy-done
  51.8 4.2 %fusion.12 = (bf16[512,1536]{1,0:T(8,128)(2,1)}, f32[512,1536]{1,0:T(8,128)S(1)}) fusion(bf16[512,1536]{1,0:T(8,128)(2,1)S(1)} %constant_dynamic-update-slice_fusion, bf16[512,768]{1,0:T(8,128)(2,1)S(1)} %copy-done, bf16[768,1536]{0,1:T(8,128)(2,1)} %all-gather.3.cloned.1.call-done), kind=kOutput, calls=%fused_computation.24 | convolution fusion | flops 1210318848 | bytes 9437184 | tf_op jit(solution)/shard_map/dot_general | solution.py:400
  56.1 1.3 constant_dynamic-slice_fusion.own_ref
  57.3 155.3 %shard_map.100 = bf16[512,768]{1,0:T(8,128)(2,1)} custom-call(bf16[2,256,1536]{2,1,0:T(8,128)(2,1)} %bitcast.11, f32[256,1536]{1,0:T(8,128)} %constant_dynamic-slice_fusion.own_ref, f32[16,8,256]{2,1,0:T(8,128)} %select_maximum_fusion.table_ref, f32[1,1536]{1,0:T(1,128)} %reshape.19.gain_mix_ref, f32[1,1536]{1,0:T(1,128)} %reshape.20.gain_out_ref, ...), custom_call_target="tpu_custom_call" | custom-call | tf_op jit(solution)/shard_map/pallas_call | solution.py:412
  212.6 2.1 copy.20
  (3 shorter events, 0.0 us)
Async XLA Ops:
  6.5 45.3 %copy-start = (bf16[512,768]{1,0:T(8,128)(2,1)S(1)}, bf16[512,768]{1,0:T(8,128)(2,1)}, u32[]{:S(2)}) copy-start(bf16[512,768]{1,0:T(8,128)(2,1)} %param.10) | copy-start | bytes 2359300
  6.5 22.0 %copy-start.1 = (bf16[512,768]{1,0:T(8,128)(2,1)S(1)}, bf16[512,768]{1,0:T(8,128)(2,1)}, u32[]{:S(2)}) copy-start(bf16[512,768]{1,0:T(8,128)(2,1)} %param.11) | copy-start | bytes 2359300
  6.5 45.3 %all-gather.3.cloned.1.call-start = ((), (), s32[]{:S(2)}) async-start(), calls=%async_computation | async-start | bytes 2506752 | tf_op jit(solution)/shard_map/all_gather | solution.py:399
Sparse Core Ops, SparseCore 0:
  9.6 42.1 all-gather.2

commit v2 on v1

--- a/solution.py
+++ b/solution.py
@@ -9,7 +9,7 @@
 
 EXPERTS = 40
 EPSILON = 1e-05
-CHUNKS = 2
+CHUNKS = 4
 MESH = pl.DeviceIdType.MESH
 
 
@@ -24,15 +24,25 @@
 
 
 def layer_kernel(
-    tp_count, chips, rows, width, local, cap, split_out,
-    parts_ref, own_ref, table_ref, gain_mix_ref, gain_out_ref, gate_hbm, up_hbm, down_hbm,
-    out_ref,
+    tp_count, chips, rows, width, local, cap, topk, inside,
+    *refs,
+):
+    if inside:
+        attn_ref, resid_ref, w_part, *refs = refs
+    else:
+        parts_ref, own_ref, *refs = refs
+    split_out = inside
+    (routed_ref, gains, gate_hbm, up_hbm, down_hbm, out_ref, *refs) = refs
+    if inside:
+        parts_ref, w_all, w_pair_send, w_pair_recv, w_send, w_recv, *refs = refs
+    (
     tokens, sums, away, from_pair, from_prev, from_next, hidden, part_in, w_gate, w_up, w_down,
     picked, pick_mats, scaled, finished,
     weight_sem, part_send, part_recv, right_send, right_recv, left_send, left_recv,
     pair_send, pair_recv, down_send, down_recv, back_send, back_recv, cross_send, cross_recv,
     out_send, out_recv,
-):
+    routed, places, shares, r_pair_send, r_pair_recv, r_send, r_recv,
+    ) = refs
     half = chips // 2
     step_rows = rows // CHUNKS
     mid = width // 2
@@ -70,14 +80,127 @@
         return pl.ds(c * step_rows, step_rows)
 
     def part_copy(k, c):
-        return to_tp(parts_ref.at[(tp + k) % tp_count, band(c)], part_in.at[k - 1, band(c)],
+        return to_tp(parts_ref.at[k - 1 if inside else (tp + k) % tp_count, band(c)], part_in.at[k - 1, band(c)],
                      part_send.at[k - 1, c], part_recv.at[k - 1, c], k)
 
-    for c in range(CHUNKS):
+    def device_at(back, which=0):
+        return chip_at((place + chips + back) % chips, chips) * 2 + (core + which - 2 * core * which)
+
+    def routes_ring(t, way):
+        held = routed.at[device_at(-way * (t - 1))]
+        return to_ep(held, routed.at[device_at(-way * (t - 1))],
+                     r_send.at[(1 - way) // 2, t - 1], r_recv.at[(1 - way) // 2, t - 1],
+                     after if way == 1 else before)
+
+    def routes_got(t, way):
+        held = routed.at[device_at(-way * t)]
+        return to_ep(held, held, r_send.at[(1 - way) // 2, t - 1], r_recv.at[(1 - way) // 2, t - 1],
+                     after if way == 1 else before)
+
+    def routes_pair(s, which):
+        held = routed.at[device_at(-s, which)]
+        return to_ep(held, held, r_pair_send.at[s], r_pair_recv.at[s], pair)
+
+    if inside:
+        columns = w_part.shape[0]
+
+        def w_rows(device, t, way):
+            if t < half:
+                return w_all.at[pl.ds(device * columns, columns)]
+            part = columns // 2
+            return w_all.at[pl.ds(device * columns + (0 if way == 1 else part), part)]
+
+        def w_ring(t, way, got=0):
+            held = w_rows(device_at(-way * (t - 1 + got)), t, way)
+            return to_ep(held, held, w_send.at[(1 - way) // 2, t - 1], w_recv.at[(1 - way) // 2, t - 1],
+                         after if way == 1 else before)
+
+        def w_pair(s, which):
+            held = w_all.at[pl.ds(device_at(-s, which) * columns, columns)]
+            return to_ep(held, held, w_pair_send.at[s], w_pair_recv.at[s], pair)
+
+        w_all[pl.ds(ep * columns, columns), :] = w_part[...]
+    routed[ep] = routed_ref[...]
+    for t in range(1, half + 1):
+        for way in (1, -1):
+            if t > 1 and inside:
+                w_ring(t - 1, way, 1).wait_recv()
+            if inside:
+                w_ring(t, way).start()
+        if inside:
+            if t == 1:
+                w_pair(0, 0).start()
+            else:
+                w_pair(t - 1, 0).start()
+                w_pair(chips - t + 1, 0).start()
+        for way in (1, -1):
+            if t > 1:
+                routes_got(t - 1, way).wait_recv()
+            if t < half or way == 1:
+                routes_ring(t, way).start()
+        if t == 1:
+            routes_pair(0, 0).start()
+        else:
+            routes_pair(t - 1, 0).start()
+            routes_pair(chips - t + 1, 0).start()
+    if inside:
+        w_ring(half, 1, 1).wait_recv()
+        w_ring(half, -1, 1).wait_recv()
+        w_pair(half, 0).start()
+    routes_got(half, 1).wait_recv()
+    routes_pair(half, 0).start()
+    if inside:
+        for s in range(chips):
+            w_pair(s, 1).wait_recv()
+
+        part_width = width // tp_count
+        mine = pl.ds(pl.multiple_of(tp * part_width, 128), part_width)
+
+        def project(k, c):
+            first = ((tp + k) % tp_count) * rows + c * step_rows
+            from_rows = pl.ds(pl.multiple_of(first, step_rows), step_rows)
+            hidden[band(c), :] = lax.dot_general(
+                attn_ref[from_rows, :], w_all[...], (((1,), (1,)), ((), ())),
+                preferred_element_type=jnp.float32)
+            hidden[band(c), mine] = hidden[band(c), mine] + resid_ref[from_rows, :].astype(jnp.float32)
+
         for k in range(1, tp_count):
-            part_copy(k, c).start()
+            for c in range(CHUNKS):
+                project(k, c)
+                parts_ref[k - 1, band(c), :] = hidden[band(c), :].astype(jnp.bfloat16)
+                part_copy(k, c).start()
+        for c in range(CHUNKS):
+            project(0, c)
+    else:
+        for c in range(CHUNKS):
+            for k in range(1, tp_count):
+                part_copy(k, c).start()
     for load in loads:
         load.start()
+    for s in range(chips):
+        routes_pair(s, 1).wait_recv()
+
+    earlier = jnp.where(
+        lax.broadcasted_iota(jnp.int32, (rows, rows), 0) < lax.broadcasted_iota(jnp.int32, (rows, rows), 1),
+        1.0, 0.0).astype(jnp.bfloat16)
+
+    def lay_out(block, carry):
+        names = routed[block, pl.ds(0, topk), :]
+        weights = routed[block, pl.ds(topk, topk), :]
+        hits = []
+        for f in range(local):
+            slot = ep * local + f
+            expert = jnp.where(slot < EXPERTS, slot, -1).astype(jnp.float32)
+            named = names == expert
+            hits.append(jnp.max(jnp.where(named, 1.0, 0.0), axis=0, keepdims=True))
+            shares[block, pl.ds(f, 1), :] = jnp.sum(jnp.where(named, weights, 0.0), axis=0, keepdims=True)
+        hits = hits + [jnp.zeros((1, rows), jnp.float32)] * (8 - local)
+        hits = jnp.concatenate(hits, axis=0)
+        rank = jnp.dot(hits.astype(jnp.bfloat16), earlier, preferred_element_type=jnp.float32)
+        places[block] = jnp.where(hits > 0.5, rank, -1.0)
+        return carry
+
+    lax.fori_loop(0, 2 * chips, lay_out, 0)
 
     def right_copy(t, c):
         return to_ep(tokens.at[t - 1, 0, band(c)], tokens.at[t, 0, band(c)],
@@ -101,10 +224,10 @@
 
     small = min(32, step_rows)
 
-    def norm_rows(at, gain_ref, add):
+    def norm_rows(at, which, add):
         value = add(at)
         scale = lax.rsqrt(jnp.mean(value * value, axis=1, keepdims=True) + EPSILON)
-        return value, (value * scale * gain_ref[...]).astype(jnp.bfloat16)
+        return value, (value * scale * gains[pl.ds(which, 1), :]).astype(jnp.bfloat16)
 
     for c in range(CHUNKS):
         for k in range(1, tp_count):
@@ -114,12 +237,12 @@
             at = pl.ds(pl.multiple_of(c * step_rows + i * small, small), small)
 
             def add(at):
-                value = own_ref[at, :]
+                value = (hidden if inside else own_ref)[at, :]
                 for k in range(1, tp_count):
                     value = value + part_in[k - 1, at, :].astype(jnp.float32)
                 return value
 
-            value, normed = norm_rows(at, gain_mix_ref, add)
+            value, normed = norm_rows(at, 0, add)
             hidden[at, :] = value
             tokens[0, 0, at, :] = normed
             return carry
@@ -142,8 +265,8 @@
             at = pl.ds(pl.multiple_of(f * cap, cap), cap)
             columns = []
             for b, (slot, which, _) in enumerate(blocks):
-                place_row = table_ref[where[b], pl.ds(f, 1), :]
-                gate_row = table_ref[where[b], pl.ds(local + f, 1), :]
+                place_row = places[where[b], pl.ds(f, 1), :]
+                gate_row = shares[where[b], pl.ds(f, 1), :]
                 index = lax.broadcasted_iota(jnp.int32, (cap, rows), 0).astype(jnp.float32)
                 hit = index == place_row
                 columns.append(jnp.sum(jnp.where(hit, gate_row, 0.0), axis=1, keepdims=True))
@@ -315,7 +438,7 @@
                     value = value + part[at, :].astype(jnp.float32)
                 return value
 
-            _, done = norm_rows(at, gain_out_ref, add)
+            _, done = norm_rows(at, 1, add)
             if split_out:
                 for r in range(tp_count):
                     finished[r, at, :] = done[:, r * part_width:(r + 1) * part_width]
@@ -365,13 +488,22 @@
     lax.fori_loop(0, chips, drain_pair, 0)
     cross_copy(half, 2 * turn_a).wait_send()
     cross_copy(0, 2 * turn_b).wait_send()
+    for t in range(1, half + 1):
+        for way in (1, -1):
+            if t < half or way == 1:
+                routes_ring(t, way).wait_send()
+            if inside:
+                w_ring(t, way).wait_send()
+    for s in range(chips):
+        routes_pair(s, 0).wait_send()
+        if inside:
+            w_pair(s, 0).wait_send()
 
 
 def per_device(attn, resid, w_out, gain_mix, gain_out, routes, gates, w_gate, w_up, w_down):
     tp_count = lax.axis_size("tp")
     tp_rank = lax.axis_index("tp")
     ep_count = lax.axis_size("ep")
-    ep_rank = lax.axis_index("ep")
     tok_dev, width_part = attn.shape
     width = width_part * tp_count
     rows = tok_dev // tp_count
@@ -380,41 +512,39 @@
     cap = rows * topk // 32
     chips = ep_count // 2
     half = chips // 2
-    split_out = width_part % 128 == 0
 
     my_routes = lax.dynamic_slice_in_dim(routes, tp_rank * rows, rows, 0)
     my_gates = lax.dynamic_slice_in_dim(gates, tp_rank * rows, rows, 0)
     both = jnp.concatenate([my_routes.T.astype(jnp.float32), my_gates.T], axis=0)
-    both = lax.all_gather(both, "ep", axis=0)
-    slot = ep_rank * local + jnp.arange(local, dtype=jnp.int32)
-    expert = jnp.where(slot < EXPERTS, slot, -1).astype(jnp.float32)
-    named = both[:, None, :topk, :] == expert[None, :, None, None]
-    hit = jnp.any(named, axis=2)
-    weight = jnp.sum(jnp.where(named, both[:, None, topk:, :], 0.0), axis=2)
-    earlier = jnp.triu(jnp.ones((rows, rows), jnp.bfloat16), 1)
-    rank = jnp.einsum("bfi,ij->bfj", hit.astype(jnp.bfloat16), earlier, preferred_element_type=jnp.float32)
-    table = jnp.concatenate([jnp.where(hit, rank, -1.0), weight], axis=1)
-    table = jnp.pad(table, ((0, 0), (0, -(2 * local) % 8), (0, 0)))
-
-    columns = lax.all_gather(w_out, "ep", axis=1, tiled=True)
-    part = jnp.dot(attn, columns, preferred_element_type=jnp.float32)
-    spread = lax.dynamic_update_slice(jnp.zeros((tok_dev, width), resid.dtype), resid, (0, tp_rank * width_part))
-    part = part + spread.astype(jnp.float32)
-    own = lax.dynamic_slice_in_dim(part, tp_rank * rows, rows, 0)
-    parts = part.astype(jnp.bfloat16).reshape(tp_count, rows, width)
+    gains = jnp.stack([gain_mix, gain_out])
+    inside = width_part % 128 == 0 and w_out.shape[1] % 32 == 0
+    if inside:
+        first = (attn, resid, w_out.T)
+    else:
+        columns = lax.all_gather(w_out, "ep", axis=1, tiled=True)
+        part = jnp.dot(attn, columns, preferred_element_type=jnp.float32)
+        spread = lax.dynamic_update_slice(
+            jnp.zeros((tok_dev, width), resid.dtype), resid, (0, tp_rank * width_part))
+        part = part + spread.astype(jnp.float32)
+        own = lax.dynamic_slice_in_dim(part, tp_rank * rows, rows, 0)
+        first = (part.astype(jnp.bfloat16).reshape(tp_count, rows, width), own)
 
     bf16, f32 = jnp.bfloat16, jnp.float32
     vmem = pl.BlockSpec(memory_space=pltpu.VMEM)
     anywhere = pl.BlockSpec(memory_space=pl.ANY)
     dma = pltpu.SemaphoreType.DMA
     others = tp_count - 1
-    out_shape = (tok_dev, width_part) if split_out else (rows, width)
+    out_shape = (tok_dev, width_part) if inside else (rows, width)
     result = pl.pallas_call(
-        functools.partial(layer_kernel, tp_count, chips, rows, width, local, cap, split_out),
+        functools.partial(layer_kernel, tp_count, chips, rows, width, local, cap, topk, inside),
         out_shape=jax.ShapeDtypeStruct(out_shape, bf16),
-        in_specs=[vmem] * 5 + [anywhere] * 3,
+        in_specs=[vmem] * (len(first) + 2) + [anywhere] * 3,
         out_specs=vmem,
-        scratch_shapes=[
+        scratch_shapes=([
+            pltpu.VMEM((others, rows, width), bf16),
+            pltpu.VMEM((width, width_part), bf16),
+            dma((chips,)), dma((chips,)), dma((2, half)), dma((2, half)),
+        ] if inside else []) + [
             pltpu.VMEM((chips, 2, rows, width), bf16),
             pltpu.VMEM((chips, rows, width), bf16),
             pltpu.VMEM((4, rows, width), bf16),
@@ -439,11 +569,15 @@
             dma((half, CHUNKS)), dma((half, CHUNKS)),
             dma((chips,)), dma((chips,)),
             dma((others, CHUNKS)), dma((others, CHUNKS)),
+            pltpu.VMEM((ep_count, 2 * topk, rows), f32),
+            pltpu.VMEM((ep_count, 8, rows), f32),
+            pltpu.VMEM((ep_count, 8, rows), f32),
+            dma((chips,)), dma((chips,)), dma((2, half)), dma((2, half)),
         ],
         compiler_params=pltpu.CompilerParams(
             collective_id=0, has_side_effects=True, vmem_limit_bytes=63 * 1024 * 1024),
-    )(parts, own, table, gain_mix.reshape(1, width), gain_out.reshape(1, width), w_gate, w_up, w_down)
-    if split_out:
+    )(*first, both, gains, w_gate, w_up, w_down)
+    if inside:
         return result
     return lax.all_to_all(result, "tp", split_axis=1, concat_axis=0, tiled=True)
 

time: 224 us -> 180 us (0.80)
  waiting for transfers between devices: 23.9 us -> 0 us
  Pallas kernels: 155 us -> 172 us
  blocking collectives: 15.8 us -> 0 us
  between operations: 13.4 us -> 0.01 us
  matrix products: 4.38 us -> 0 us
  local copies, waits for them, and re-layouts: 6.81 us -> 3.49 us
    all_gather x1 -> x0, waiting for transfers between devices: 23.2 us -> none  [per_device(): columns = lax.all_gather(w_out, 'ep', axis=1, tiled=True)]
    pallas_call x1, Pallas kernels: 155 us -> 172 us  [per_device(): pl.pallas_call(functools.partial(layer_kernel, tp_count, chips, rows, wid...]
    all_gather x1 -> x0, blocking collectives: 15.8 us -> none  [per_device(): both = lax.all_gather(both, 'ep', axis=0)]
    dot_general x2 -> x0, matrix products: 4.38 us -> none  [the longest x1 4.24 us: per_device(): part = jnp.dot(attn, columns, preferred_element_type=jnp.float32)]
    reshape x2 -> x0, local copies, waits for them, and re-layouts: 2.59 us -> none  [the longest x1 1.29 us: per_device(): gain_mix.reshape(1, width)]
  transfers between devices with their start and end apart: 1 -> 0, of which waited for: 1 -> 0; matrix products, arithmetic and copies ran while one was open for 2% -> 0% of each run, Pallas kernels for 0% -> 0%
where the time goes in v2:
time: 180 us; the launch traced here: 177 us
  Pallas kernels  172 us (96%)
  local copies, waits for them, and re-layouts  3.49 us (2%)
  other arithmetic  1.92 us (1%)
    pallas_call x1, Pallas kernels, per_device(): pl.pallas_call(functools.partial(layer_kernel, tp_count, chips, rows, wid...  172 us

profile of v2, /device:TPU:12, one launch (start us, length us, event | category | flops | bytes accessed | tf_op | source)
XLA Modules:
  0.0 177.0 jit_solution(6077662572230733295)
XLA Ops:
  0.0 0.0 copy-start
  0.0 0.7 stack.9
  0.7 0.7 stack.10
  1.4 0.6 pad_maximum_fusion.1.refs_4_
  2.0 0.7 convert_bitcast_fusion
  2.7 0.0 copy-done
  2.7 0.6 pad_maximum_fusion.refs_3_
  3.3 171.6 %shard_map.100 = bf16[512,768]{1,0:T(8,128)(2,1)} custom-call(bf16[512,768]{1,0:T(8,128)(2,1)} %refs_0_.1, bf16[512,768]{1,0:T(8,128)(2,1)} %refs_1_.1, bf16[96,768]{1,0:T(8,128)(2,1)} %bitcast.5, f32[16,256]{1,0:T(8,128)} %pad_maximum_fusion.refs_3_, f32[2,1536]{1,0:T(2,128)} %pad_maximum_fusion.1.refs_4_, bf16[3,1536,512]{2,1,0:T(8,128)(2,1)} %refs_5_.1, ...), custom_call_target="tpu_custom_call" | custom-call | tf_op jit(solution)/shard_map/pallas_call | solution.py:538
  174.9 2.1 %copy.12 = bf16[512,768]{1,0:T(8,128)(2,1)} copy(bf16[512,768]{1,0:T(8,128)(2,1)} %shard_map.100) | data formatting | bytes 1572864
  (1 shorter events, 0.0 us)
Async XLA Ops:
  0.0 2.7 %copy-start = (f32[512,8]{0,1:T(8,128)S(1)}, f32[512,8]{0,1:T(8,128)}, u32[]{:S(2)}) copy-start(f32[512,8]{0,1:T(8,128)} %param.16) | copy-start | bytes 49156

commit v3 on v2

--- a/solution.py
+++ b/solution.py
@@ -32,7 +32,7 @@
     else:
         parts_ref, own_ref, *refs = refs
     split_out = inside
-    (routed_ref, gains, gate_hbm, up_hbm, down_hbm, out_ref, *refs) = refs
+    (routed_ref, gain_mix, gain_out, gate_hbm, up_hbm, down_hbm, out_ref, *refs) = refs
     if inside:
         parts_ref, w_all, w_pair_send, w_pair_recv, w_send, w_recv, *refs = refs
     (
@@ -41,8 +41,9 @@
     weight_sem, part_send, part_recv, right_send, right_recv, left_send, left_recv,
     pair_send, pair_recv, down_send, down_recv, back_send, back_recv, cross_send, cross_recv,
     out_send, out_recv,
-    routed, places, shares, r_pair_send, r_pair_recv, r_send, r_recv,
+    routed, places, shares, r_pair_send, r_pair_recv, r_send, r_recv, early_send, early_recv,
     ) = refs
+    gain_refs = (gain_mix, gain_out)
     half = chips // 2
     step_rows = rows // CHUNKS
     mid = width // 2
@@ -177,6 +178,55 @@
                 part_copy(k, c).start()
     for load in loads:
         load.start()
+    def right_copy(t, c):
+        return to_ep(tokens.at[t - 1, 0, band(c)], tokens.at[t, 0, band(c)],
+                     right_send.at[t - 1, c], right_recv.at[t - 1, c], after)
+
+    def left_copy(t, c):
+        return to_ep(tokens.at[(chips - t + 1) % chips, 0, band(c)], tokens.at[chips - t, 0, band(c)],
+                     left_send.at[t - 1, c], left_recv.at[t - 1, c], before)
+
+    def right_last(c):
+        return to_ep(tokens.at[half - 1, 0, band(c), pl.ds(0, mid)], tokens.at[half, 0, band(c), pl.ds(0, mid)],
+                     right_send.at[half - 1, c], right_recv.at[half - 1, c], after)
+
+    def left_last(c):
+        return to_ep(tokens.at[half + 1, 0, band(c), pl.ds(mid, mid)], tokens.at[half, 0, band(c), pl.ds(mid, mid)],
+                     left_send.at[half - 1, c], left_recv.at[half - 1, c], before)
+
+    def pair_copy(s, c):
+        return to_ep(tokens.at[s, 0, band(c)], tokens.at[s, 1, band(c)],
+                     pair_send.at[s, c], pair_recv.at[s, c], pair)
+
+    small = min(32, step_rows)
+
+    def norm_rows(at, which, add):
+        value = add(at)
+        scale = lax.rsqrt(jnp.mean(value * value, axis=1, keepdims=True) + EPSILON)
+        return value, (value * scale * gain_refs[which][...][None, :]).astype(jnp.bfloat16)
+
+    for c in range(CHUNKS):
+        for k in range(1, tp_count):
+            part_copy(k, c).wait_recv()
+
+        def mix(i, carry):
+            at = pl.ds(pl.multiple_of(c * step_rows + i * small, small), small)
+
+            def add(at):
+                value = (hidden if inside else own_ref)[at, :]
+                for k in range(1, tp_count):
+                    value = value + part_in[k - 1, at, :].astype(jnp.float32)
+                return value
+
+            value, normed = norm_rows(at, 0, add)
+            hidden[at, :] = value
+            tokens[0, 0, at, :] = normed
+            return carry
+
+        lax.fori_loop(0, step_rows // small, mix, 0)
+        right_copy(1, c).start()
+        left_copy(1, c).start()
+        pair_copy(0, c).start()
     for s in range(chips):
         routes_pair(s, 1).wait_recv()
 
@@ -202,55 +252,6 @@
 
     lax.fori_loop(0, 2 * chips, lay_out, 0)
 
-    def right_copy(t, c):
-        return to_ep(tokens.at[t - 1, 0, band(c)], tokens.at[t, 0, band(c)],
-                     right_send.at[t - 1, c], right_recv.at[t - 1, c], after)
-
-    def left_copy(t, c):
-        return to_ep(tokens.at[(chips - t + 1) % chips, 0, band(c)], tokens.at[chips - t, 0, band(c)],
-                     left_send.at[t - 1, c], left_recv.at[t - 1, c], before)
-
-    def right_last(c):
-        return to_ep(tokens.at[half - 1, 0, band(c), pl.ds(0, mid)], tokens.at[half, 0, band(c), pl.ds(0, mid)],
-                     right_send.at[half - 1, c], right_recv.at[half - 1, c], after)
-
-    def left_last(c):
-        return to_ep(tokens.at[half + 1, 0, band(c), pl.ds(mid, mid)], tokens.at[half, 0, band(c), pl.ds(mid, mid)],
-                     left_send.at[half - 1, c], left_recv.at[half - 1, c], before)
-
-    def pair_copy(s, c):
-        return to_ep(tokens.at[s, 0, band(c)], tokens.at[s, 1, band(c)],
-                     pair_send.at[s, c], pair_recv.at[s, c], pair)
-
-    small = min(32, step_rows)
-
-    def norm_rows(at, which, add):
-        value = add(at)
-        scale = lax.rsqrt(jnp.mean(value * value, axis=1, keepdims=True) + EPSILON)
-        return value, (value * scale * gains[pl.ds(which, 1), :]).astype(jnp.bfloat16)
-
-    for c in range(CHUNKS):
-        for k in range(1, tp_count):
-            part_copy(k, c).wait_recv()
-
-        def mix(i, carry):
-            at = pl.ds(pl.multiple_of(c * step_rows + i * small, small), small)
-
-            def add(at):
-                value = (hidden if inside else own_ref)[at, :]
-                for k in range(1, tp_count):
-                    value = value + part_in[k - 1, at, :].astype(jnp.float32)
-                return value
-
-            value, normed = norm_rows(at, 0, add)
-            hidden[at, :] = value
-            tokens[0, 0, at, :] = normed
-            return carry
-
-        lax.fori_loop(0, step_rows // small, mix, 0)
-        right_copy(1, c).start()
-        left_copy(1, c).start()
-        pair_copy(0, c).start()
     for load in loads:
         load.wait()
 
@@ -336,19 +337,6 @@
 
     lax.fori_loop(1, half, step, 0)
 
-    for c in range(CHUNKS):
-        right_last(c).wait_recv()
-        left_last(c).wait_recv()
-        pair_copy(half, c).start()
-    for c in range(CHUNKS):
-        pair_copy(half, c).wait_recv()
-    turn_a, turn_b = half % 2, (half - 1) % 2
-    if half > 2:
-        cross_copy(half - 2, 2 * turn_a).wait_send()
-        cross_copy(chips - half + 2, 2 * turn_a + 1).wait_send()
-    experts([(half, 0, sums.at[half]), (half, 1, away.at[2 * turn_a])])
-    cross_copy(half, 2 * turn_a).start()
-
     def add_rows(s, at, extra, columns=slice(None)):
         def body(i, carry):
             here = pl.ds(pl.multiple_of(at + i * small, small), small)
@@ -376,6 +364,45 @@
         return to_ep(sums.at[t, band(c)], from_next.at[t - 1, band(c)],
                      back_send.at[t - 1, c], back_recv.at[t - 1, c], before)
 
+    last = half - 1
+
+    def down_late(c):
+        return to_ep(sums.at[chips - last, band(c), pl.ds(0, mid)], from_prev.at[last - 1, band(c), pl.ds(0, mid)],
+                     down_send.at[last - 1, c], down_recv.at[last - 1, c], after)
+
+    def back_late(c):
+        return to_ep(sums.at[last, band(c), pl.ds(mid, mid)], from_next.at[last - 1, band(c), pl.ds(mid, mid)],
+                     back_send.at[last - 1, c], back_recv.at[last - 1, c], before)
+
+    def down_early(c):
+        return to_ep(sums.at[chips - last, band(c), pl.ds(mid, mid)], from_prev.at[last - 1, band(c), pl.ds(mid, mid)],
+                     early_send.at[0, c], early_recv.at[0, c], after)
+
+    def back_early(c):
+        return to_ep(sums.at[last, band(c), pl.ds(0, mid)], from_next.at[last - 1, band(c), pl.ds(0, mid)],
+                     early_send.at[1, c], early_recv.at[1, c], before)
+
+    cross_copy(last, 0).wait_recv()
+    cross_copy(chips - last, 0).wait_recv()
+    for c in range(CHUNKS):
+        add_rows(chips - last, c * step_rows, None, pl.ds(mid, mid))
+        down_early(c).start()
+        add_rows(last, c * step_rows, None, pl.ds(0, mid))
+        back_early(c).start()
+
+    for c in range(CHUNKS):
+        right_last(c).wait_recv()
+        left_last(c).wait_recv()
+        pair_copy(half, c).start()
+    for c in range(CHUNKS):
+        pair_copy(half, c).wait_recv()
+    turn_a, turn_b = half % 2, (half - 1) % 2
+    if half > 2:
+        cross_copy(half - 2, 2 * turn_a).wait_send()
+        cross_copy(chips - half + 2, 2 * turn_a + 1).wait_send()
+    experts([(half, 0, sums.at[half]), (half, 1, away.at[2 * turn_a])])
+    cross_copy(half, 2 * turn_a).start()
+
     cross_copy(half, 2 * turn_a).wait_recv()
     for c in range(CHUNKS):
         add_rows(half, c * step_rows, None)
@@ -389,28 +416,40 @@
     experts([(0, 0, sums.at[0]), (0, 1, away.at[2 * turn_b])])
     cross_copy(0, 2 * turn_b).start()
 
-    last = half - 1
-    cross_copy(last, 0).wait_recv()
-    cross_copy(chips - last, 0).wait_recv()
     for c in range(CHUNKS):
         down_first(c).wait_recv()
         add_rows(chips - last, c * step_rows, from_prev.at[last], pl.ds(0, mid))
-        add_rows(chips - last, c * step_rows, None, pl.ds(mid, mid))
-        down_copy(last, c).start()
+        down_late(c).start()
         back_first(c).wait_recv()
-        add_rows(last, c * step_rows, None, pl.ds(0, mid))
         add_rows(last, c * step_rows, from_next.at[last], pl.ds(mid, mid))
-        back_copy(last, c).start()
+        back_late(c).start()
+
+    def halves_in(c):
+        down_early(c).wait_recv()
+        back_early(c).wait_recv()
+        down_late(c).wait_recv()
+        back_late(c).wait_recv()
 
     def sum_step(i, carry):
         t = half - 2 - i
         cross_copy(t, 0).wait_recv()
         cross_copy(chips - t, 0).wait_recv()
         for c in range(CHUNKS):
-            down_copy(t + 1, c).wait_recv()
+            @pl.when(i == 0)
+            def _():
+                halves_in(c)
+
+            @pl.when(i > 0)
+            def _():
+                down_copy(t + 1, c).wait_recv()
+
             add_rows(chips - t, c * step_rows, from_prev.at[t])
             down_copy(t, c).start()
-            back_copy(t + 1, c).wait_recv()
+
+            @pl.when(i > 0)
+            def _():
+                back_copy(t + 1, c).wait_recv()
+
             add_rows(t, c * step_rows, from_next.at[t])
             back_copy(t, c).start()
         return carry
@@ -426,8 +465,11 @@
                      out_send.at[k - 1, c], out_recv.at[k - 1, c], k)
 
     for c in range(CHUNKS):
-        down_copy(1, c).wait_recv()
-        back_copy(1, c).wait_recv()
+        if last == 1:
+            halves_in(c)
+        else:
+            down_copy(1, c).wait_recv()
+            back_copy(1, c).wait_recv()
 
         def close(i, carry):
             at = pl.ds(pl.multiple_of(c * step_rows + i * small, small), small)
@@ -468,17 +510,26 @@
         left_last(c).wait_send()
         down_first(c).wait_send()
         back_first(c).wait_send()
+        for copy in (down_early, back_early, down_late, back_late):
+            copy(c).wait_send()
 
     def drain(i, carry):
         t = i + 1
         for c in range(CHUNKS):
             right_copy(t, c).wait_send()
             left_copy(t, c).wait_send()
+        return carry
+
+    lax.fori_loop(0, half - 1, drain, 0)
+
+    def drain_sums(i, carry):
+        t = i + 1
+        for c in range(CHUNKS):
             down_copy(t, c).wait_send()
             back_copy(t, c).wait_send()
         return carry
 
-    lax.fori_loop(0, half - 1, drain, 0)
+    lax.fori_loop(0, half - 2, drain_sums, 0)
 
     def drain_pair(s, carry):
         for c in range(CHUNKS):
@@ -516,7 +567,6 @@
     my_routes = lax.dynamic_slice_in_dim(routes, tp_rank * rows, rows, 0)
     my_gates = lax.dynamic_slice_in_dim(gates, tp_rank * rows, rows, 0)
     both = jnp.concatenate([my_routes.T.astype(jnp.float32), my_gates.T], axis=0)
-    gains = jnp.stack([gain_mix, gain_out])
     inside = width_part % 128 == 0 and w_out.shape[1] % 32 == 0
     if inside:
         first = (attn, resid, w_out.T)
@@ -538,7 +588,7 @@
     result = pl.pallas_call(
         functools.partial(layer_kernel, tp_count, chips, rows, width, local, cap, topk, inside),
         out_shape=jax.ShapeDtypeStruct(out_shape, bf16),
-        in_specs=[vmem] * (len(first) + 2) + [anywhere] * 3,
+        in_specs=[vmem] * (len(first) + 3) + [anywhere] * 3,
         out_specs=vmem,
         scratch_shapes=([
             pltpu.VMEM((others, rows, width), bf16),
@@ -573,10 +623,11 @@
             pltpu.VMEM((ep_count, 8, rows), f32),
             pltpu.VMEM((ep_count, 8, rows), f32),
             dma((chips,)), dma((chips,)), dma((2, half)), dma((2, half)),
+            dma((2, CHUNKS)), dma((2, CHUNKS)),
         ],
         compiler_params=pltpu.CompilerParams(
             collective_id=0, has_side_effects=True, vmem_limit_bytes=63 * 1024 * 1024),
-    )(*first, both, gains, w_gate, w_up, w_down)
+    )(*first, both, gain_mix, gain_out, w_gate, w_up, w_down)
     if inside:
         return result
     return lax.all_to_all(result, "tp", split_axis=1, concat_axis=0, tiled=True)

time: 180 us -> 169 us (0.939)
  Pallas kernels: 172 us -> 163 us
    pallas_call x1, Pallas kernels: 172 us -> 163 us  [per_device(): pl.pallas_call(functools.partial(layer_kernel, tp_count, chips, rows, wid...]
where the time goes in v3:
time: 169 us; the launch traced here: 166 us
  Pallas kernels  163 us (96%)
  local copies, waits for them, and re-layouts  2.07 us (1%)
    pallas_call x1, Pallas kernels, per_device(): pl.pallas_call(functools.partial(layer_kernel, tp_count, chips, rows, wid...  163 us

profile of v3, /device:TPU:12, one launch (start us, length us, event | category | flops | bytes accessed | tf_op | source)
XLA Modules:
  0.0 166.4 jit_solution(7403491279707946351)
XLA Ops:
  0.0 0.0 copy-start
  0.0 0.7 convert_bitcast_fusion
  0.7 0.0 copy-done
  0.7 0.6 pad_maximum_fusion.refs_3_
  1.3 163.0 %shard_map.100 = bf16[512,768]{1,0:T(8,128)(2,1)} custom-call(bf16[512,768]{1,0:T(8,128)(2,1)} %refs_0_.1, bf16[512,768]{1,0:T(8,128)(2,1)} %refs_1_.1, bf16[96,768]{1,0:T(8,128)(2,1)} %bitcast.5, f32[16,256]{1,0:T(8,128)} %pad_maximum_fusion.refs_3_, f32[1536]{0:T(1024)} %refs_4_.1, f32[1536]{0:T(1024)} %refs_5_.1, bf16[3,1536,512]{2,1,0:T(8,128)(2,1)} %refs_6_.1, ...), custom_call_target="tpu_custom_call" | custom-call | tf_op jit(solution)/shard_map/pallas_call | solution.py:588
  164.3 2.1 %copy.12 = bf16[512,768]{1,0:T(8,128)(2,1)} copy(bf16[512,768]{1,0:T(8,128)(2,1)} %shard_map.100) | data formatting | bytes 1572864
  (1 shorter events, 0.0 us)
Async XLA Ops:
  0.0 0.7 copy-start
